TPU v7x, 32 devices: a whole 2x2x4 slice. The times are simulated.
32 devices in a mesh: tile: 2 (over core), epoch: 16 (over z, y, x).
Axes of the slice: x: 2, y: 2, z: 4, core: 2. Of those that a mesh axis runs over, the one named last changes fastest.
Arguments:
- template: float32 [2, 256, 128], P('tile', 'epoch')
- science: bfloat16 [2, 128, 256, 128], P('tile', 'epoch')
- weights: float32 [2, 128, 256, 128], P('tile', 'epoch'), may hold values from 0.03 to 6.4
- shifts: int32 [128, 2], P('epoch'), may hold values from -8 to 8
- valid: int32 [2, 128], P('tile', 'epoch'), may hold values 0 or 1
- counts: int32 [2], P('tile'), may hold values from 32 to 128, as said below
Outputs:
- coadd: float32 [2, 256, 128], P('tile', 'epoch')
- coefficients: float32 [2, 128, 45], P('tile', 'epoch')
Inputs may be any that keep to these rules, and one draw needn't show every extreme that they name: `counts`: some tile has all 128 epochs observed; epochs at or after a tile's count are unused.
All inputs are finite; a program needn't handle non-finite values. No bound on the sum of `valid` on one device may be relied on, other than what follows from the above.
Results may differ from a plain program's by a relative error of at most 0.0025.
Values may be sent and summed in bfloat16 or wider, within the bound.
A program may use at most 128 MiB of HBM per device.

v0:
```python
import jax
import jax.numpy as jnp
from jax import lax
from jax.sharding import PartitionSpec as P

NB = 45
HALF = 11
SHIFT = 8
W = 128
H = 256


SIGMAS = (0.75, 1.5, 3.0)
RIDGE = 0.5


def padded_2(cells, sides, width):
    for axis, dim in sides:
        count = lax.axis_size(axis)
        ends = count - 1
        head = lax.slice_in_dim(cells, 0, width, axis=dim)
        tail = lax.slice_in_dim(cells, cells.shape[dim] - width, cells.shape[dim], axis=dim)
        cells = jnp.concatenate(
            [
                lax.ppermute(tail, axis, [(i, (i + 1) % count) for i in range(ends)]),
                cells,
                lax.ppermute(head, axis, [((i + 1) % count, i) for i in range(ends)]),
            ],
            axis=dim,
        )
    return cells


def profile(offset, sigma, power):
    ratio = offset / sigma
    values = ratio**power * jnp.exp(-0.5 * ratio * ratio)
    return jnp.where(jnp.abs(offset) <= HALF, values, 0.0)


def row_filter(width, sigma, power):
    inner = lax.broadcasted_iota(jnp.int32, (width + 2 * HALF, width), 0)
    outer = lax.broadcasted_iota(jnp.int32, (width + 2 * HALF, width), 1)
    return profile((outer + HALF - inner).astype(jnp.float32), sigma, power)


def col_filter(start, rows, height, sigma, power):
    outer = lax.broadcasted_iota(jnp.int32, (rows, height), 0) + start
    inner = lax.broadcasted_iota(jnp.int32, (rows, height), 1)
    return profile((outer - inner).astype(jnp.float32), sigma, power)


def basis_images(padded, start, rows):
    pieces = []
    for sigma in SIGMAS:
        for power in range(5):
            filtered = jnp.dot(padded, row_filter(W, sigma, power), precision=lax.Precision.HIGHEST)
            for second in range(5 - power):
                band = col_filter(start, rows, H, sigma, second)
                pieces.append(
                    jnp.dot(band, filtered, precision=lax.Precision.HIGHEST).astype(jnp.bfloat16)
                )
    return jnp.stack(pieces)


def fit_epoch(basis, image, weight):
    weighted = (basis * weight).astype(jnp.bfloat16)
    gram = lax.dot_general(
        weighted, basis, (((1,), (1,)), ((), ())), preferred_element_type=jnp.float32
    )
    gram = 0.5 * (gram + gram.T)
    proj = jnp.dot(weighted, image, preferred_element_type=jnp.float32)
    scale = jnp.sqrt(jnp.diagonal(gram) + 1e-06)
    system = gram / (scale[:, None] * scale[None, :]) + RIDGE * jnp.eye(NB, dtype=jnp.float32)
    factor = jnp.linalg.cholesky(system)
    first = lax.linalg.triangular_solve(factor, (proj / scale)[:, None], left_side=True, lower=True)
    coef = lax.linalg.triangular_solve(factor, first, left_side=True, lower=True, transpose_a=True)[
        :, 0
    ]
    model = jnp.dot((coef / scale).astype(jnp.bfloat16), basis, preferred_element_type=jnp.float32)
    return (coef, image.astype(jnp.float32) - model)


def warp(field, rise, run):
    rows = jnp.pad(field, ((SHIFT, SHIFT), (0, 0)))
    return lax.dynamic_slice(rows, (SHIFT - rise, SHIFT - run), (H, W))


def local(template, science, weights, shifts, valid, counts):
    position = lax.axis_index("epoch")
    band_rows = template.shape[1]
    epochs_here = science.shape[1]
    whole = lax.all_gather(template[0], "epoch", axis=0, tiled=True)
    centred = whole - jnp.mean(whole)
    padded = padded_2(centred, (("tile", 1),), HALF)
    own = basis_images(padded, position * band_rows, band_rows)
    basis = lax.all_gather(own, "epoch", axis=1, tiled=True)
    basis = basis.reshape(NB, H * W)
    epoch_ids = position * epochs_here + jnp.arange(epochs_here)
    live_all = (valid[0] * (epoch_ids < counts[0]).astype(jnp.int32)).astype(jnp.float32)
    coefs = []
    prods = []
    masses = []
    for epoch in range(epochs_here):
        image = science[0, epoch].reshape(H * W)
        weight = weights[0, epoch].reshape(H * W)
        live = live_all[epoch]
        coef, diff = fit_epoch(basis, image, weight)
        coefs.append(live * coef)
        prods.append(live * weights[0, epoch] * diff.reshape(H, W))
        masses.append(live * weights[0, epoch])
    stacked = jnp.stack([jnp.stack(prods), jnp.stack(masses)])
    widened = padded_2(stacked, (("tile", 3),), SHIFT)
    rises = shifts[:, 0]
    runs = shifts[:, 1]
    numer = jnp.sum(jax.vmap(warp)(widened[0], rises, runs), axis=0)
    total = jnp.sum(jax.vmap(warp)(widened[1], rises, runs), axis=0)
    numer_band, total_band = (
        lax.psum_scatter(numer, "epoch", scatter_dimension=0, tiled=True),
        lax.psum_scatter(total, "epoch", scatter_dimension=0, tiled=True),
    )
    coadd = numer_band / jnp.sqrt(1.0 + total_band)
    return (coadd[None], jnp.stack(coefs)[None])


def solution(mesh):
    in_specs = (
        P("tile", "epoch", None),
        P("tile", "epoch", None, None),
        P("tile", "epoch", None, None),
        P("epoch", None),
        P("tile", "epoch"),
        P("tile"),
    )
    out_specs = (P("tile", "epoch", None), P("tile", "epoch", None))
    return jax.shard_map(local, mesh=mesh, in_specs=in_specs, out_specs=out_specs, check_vma=False)
```

profile of v0, /device:TPU:0, one launch (start us, length us, event | category | flops | bytes accessed | tf_op | source)
XLA Modules:
  0.0 540.7 jit_solution(4242935733897130205)
XLA Ops:
  7.2 43.3 %all-gather = f32[1,256,128]{2,1,0:T(8,128)S(1)} all-gather(f32[1,16,128]{2,1,0:T(8,128)} %param.11), channel_id=2, replica_groups=mesh['tile'=2,'epoch'=16] {'epoch'}, dimensions={1}, use_global_device_ids=true | all-gather | bytes 139264 | tf_op jit(solution)/shard_map/all_gather | solution.py:92
  82.8 61.3 %all-gather.3.cloned.1.call-done = bf16[45,256,128]{2,1,0:T(8,128)(2,1)} async-done(((bf16[45,16,128]{2,1,0:T(8,128)(2,1)}), bf16[45,256,128]{2,1,0:T(8,128)(2,1)}) %all-gather.3.cloned.1.call-update) | async-done | bytes 2949136 | tf_op jit(solution)/shard_map/all_gather | solution.py:96
  144.1 11.9 %fusion.7 = (bf16[45,256,128]{2,1,0:T(8,128)(2,1)S(1)}, bf16[45,256,128]{2,1,0:T(8,128)(2,1)}, bf16[45,256,128]{2,1,0:T(8,128)(2,1)}, bf16[45,256,128]{2,1,0:T(8...) fusion(bf16[45,256,128]{2,1,0:T(8,128)(2,1)} %all-gather.3.clon, ...), kind=kLoop, calls=%fused_computation.27 | loop fusion | flops 25067520 | bytes 27590656 | tf_op jit(solution)/shard_map/convert_element_type | solution.py:66
  156.0 3.4 fusion.8
  160.7 4.1 cholesky.211
  166.2 3.4 custom-call.53
  175.0 3.4 fusion.10
  178.5 9.7 %gather_fusion.6 = f32[45]{0:T(128)S(1)} fusion(f32[45,45]{0,1:T(8,128)S(1)} %fusion.263, s32[45]{0:T(128)S(1)} %or_bitcast_fusion), kind=kCustom, calls=%fused_computation.6 | custom fusion | bytes 720 | tf_op jit(solution)/shard_map/jit(diagonal)/cond/branch_0_fun/gather | solution.py:72
  188.5 4.1 cholesky.200
  194.0 3.4 custom-call.51
  202.5 3.4 fusion.12
  207.2 4.1 cholesky.189
  212.7 3.4 custom-call.49
  221.3 3.4 fusion.14
  226.1 4.1 cholesky.178
  231.5 3.4 custom-call.47
  240.0 3.8 fusion.16
  245.2 4.1 cholesky.167
  250.6 3.4 custom-call.45
  259.1 3.4 fusion.18
  263.9 4.1 cholesky.156
  269.3 3.4 custom-call.43
  277.9 3.4 fusion.20
  282.7 4.1 cholesky.145
  288.1 3.4 custom-call.41
  296.6 3.6 fusion.22
  301.6 4.1 cholesky.134
  307.0 3.4 custom-call.39
  345.8 3.5 pad_maximum_fusion
  351.3 29.7 %while.3 = (s32[]{:T(128)}, f32[8,272,144]{2,1,0:T(8,128)}, s32[8,3]{0,1:T(4,128)S(1)}, f32[8,256,128]{2,1,0:T(8,128)S(1)}, s32[]{:T(128)}) while((s32[]{:T(128)}, f32[8,272,144]{2,1,0:T(8,128)}, s32[8,3]{0,1:T(4,128)S(1)}, f32[8,256,128]{2,1,0:T(8,128)S(1)}, s32[]{:T(128)}) %tuple.84), condition=%wide.while_cond.1, body=%wide.while_body.1.sunk | while | flops 2 | bytes 262273 | solution.py:85
  352.0 3.0 dynamic-slice_dynamic-update-slice_fusion.5
  355.7 3.0 dynamic-slice_dynamic-update-slice_fusion.5
  359.4 3.0 dynamic-slice_dynamic-update-slice_fusion.5
  363.1 3.0 dynamic-slice_dynamic-update-slice_fusion.5
  366.8 3.0 dynamic-slice_dynamic-update-slice_fusion.5
  370.5 3.0 dynamic-slice_dynamic-update-slice_fusion.5
  374.2 3.0 dynamic-slice_dynamic-update-slice_fusion.5
  377.9 3.0 dynamic-slice_dynamic-update-slice_fusion.5
  383.4 29.7 %while.2 = (s32[]{:T(128)}, f32[8,272,144]{2,1,0:T(8,128)}, s32[8,3]{0,1:T(4,128)S(1)}, f32[8,256,128]{2,1,0:T(8,128)S(1)}, s32[]{:T(128)}) while((s32[]{:T(128)}, f32[8,272,144]{2,1,0:T(8,128)}, s32[8,3]{0,1:T(4,128)S(1)}, f32[8,256,128]{2,1,0:T(8,128)S(1)}, s32[]{:T(128)}) %tuple.93), condition=%wide.while_cond, body=%wide.while_body.sunk | while | flops 2 | bytes 262273 | solution.py:85
  384.1 3.0 dynamic-slice_dynamic-update-slice_fusion.4
  387.8 3.0 dynamic-slice_dynamic-update-slice_fusion.4
  391.5 3.0 dynamic-slice_dynamic-update-slice_fusion.4
  395.2 3.0 dynamic-slice_dynamic-update-slice_fusion.4
  402.7 3.0 dynamic-slice_dynamic-update-slice_fusion.4
  406.4 3.0 dynamic-slice_dynamic-update-slice_fusion.4
  410.1 3.0 dynamic-slice_dynamic-update-slice_fusion.4
  416.9 40.8 %reduce-scatter.5.cloned.1.call-done = f32[16,128]{1,0:T(8,128)} async-done(((f32[256,128]{1,0:T(8,128)}), f32[16,128]{1,0:T(8,128)}) %reduce-scatter.5.cloned.1.call-update) | async-done | bytes 8208 | tf_op jit(solution)/shard_map/reduce_scatter | solution.py:119
  457.7 74.7 %reduce-scatter.3.cloned.1.call-done = f32[16,128]{1,0:T(8,128)} async-done(((f32[256,128]{1,0:T(8,128)}), f32[16,128]{1,0:T(8,128)}) %reduce-scatter.3.cloned.1.call-update) | async-done | bytes 8208 | tf_op jit(solution)/shard_map/reduce_scatter | solution.py:118
  (355 shorter events, 144.9 us)
Async XLA Ops:
  7.2 136.9 %all-gather.3.cloned.1.call-start = ((), (), s32[]{:S(2)}) async-start(), calls=%async_computation.2 | async-start | bytes 3133440 | tf_op jit(solution)/shard_map/all_gather | solution.py:96
  51.9 2.6 collective-permute-start
  53.2 3.2 collective-permute-start.1
  62.6 12.2 %copy-start.19 = (bf16[1,8,256,128]{3,2,1,0:T(8,128)(2,1)S(1)}, bf16[1,8,256,128]{3,2,1,0:T(8,128)(2,1)}, u32[]{:S(2)}) copy-start(bf16[1,8,256,128]{3,2,1,0:T(8,128)(2,1)} %param.12) | copy-start | bytes 1572868
  67.6 13.7 %copy-start.30 = (s32[8,2]{0,1:T(2,128)S(1)}, s32[8,2]{0,1:T(2,128)}, u32[]{:S(2)}) copy-start(s32[8,2]{0,1:T(2,128)} %param.14) | copy-start | bytes 196
  67.6 13.7 %copy-start.31 = (s32[1,8]{1,0:T(1,128)S(1)}, s32[1,8]{1,0:T(1,128)}, u32[]{:S(2)}) copy-start(s32[1,8]{1,0:T(1,128)} %param.15) | copy-start | bytes 100
  67.6 14.4 %copy-start.16 = (f32[1,8,256,128]{3,2,1,0:T(8,128)S(1)}, f32[1,8,256,128]{3,2,1,0:T(8,128)}, u32[]{:S(2)}) copy-start(f32[1,8,256,128]{3,2,1,0:T(8,128)} %param.13) | copy-start | bytes 3145732
  73.8 0.7 copy-start.21
  74.5 383.2 %reduce-scatter.5.cloned.1.call-start = ((), (), s32[]{:S(2)}) async-start(), calls=%async_computation.4 | async-start | bytes 139264 | tf_op jit(solution)/shard_map/reduce_scatter | solution.py:119
  144.1 11.9 %copy-start = (bf16[45,256,128]{2,1,0:T(8,128)(2,1)S(1)}, bf16[45,256,128]{2,1,0:T(8,128)(2,1)}, u32[]{:S(2)}) copy-start(bf16[45,256,128]{2,1,0:T(8,128)(2,1)} %all-gather.3.cloned.1.call-done) | copy-start | bytes 8847364
  170.0 2.1 copy-start.29
  172.0 1.8 copy-start.15
  173.0 2.1 copy-start.1
  197.4 2.1 copy-start.28
  199.5 1.8 copy-start.14
  200.4 2.1 copy-start.2
  216.1 2.1 copy-start.27
  218.2 1.8 copy-start.13
  219.3 2.0 copy-start.3
  235.0 2.1 copy-start.26
  237.0 1.8 copy-start.12
  238.0 2.1 copy-start.4
  254.1 2.1 copy-start.25
  256.1 1.8 copy-start.11
  257.0 2.1 copy-start.5
  272.8 2.1 copy-start.24
  274.8 1.8 copy-start.10
  275.9 2.0 copy-start.6
  291.6 2.1 copy-start.23
  293.6 1.8 copy-start.9
  294.6 2.1 copy-start.7
  310.5 2.1 copy-start.22
  312.5 1.8 copy-start.8
  320.0 2.3 copy-start.17
  320.0 2.3 copy-start.20
  328.0 6.7 %copy-start.18 = (f32[8,256,128]{2,1,0:T(8,128)}, f32[8,256,128]{2,1,0:T(8,128)S(1)}, u32[]{:S(2)}) copy-start(f32[8,256,128]{2,1,0:T(8,128)S(1)} %get-tuple-element.63) | copy-start | bytes 3145732
  336.8 5.0 collective-permute-start.2
  339.3 3.6 collective-permute-start.3
  381.7 150.7 %reduce-scatter.3.cloned.1.call-start = ((), (), s32[]{:S(2)}) async-start(), calls=%async_computation.3 | async-start | bytes 139264 | tf_op jit(solution)/shard_map/reduce_scatter | solution.py:118
Sparse Core Ops, SparseCore 0:
  74.6 69.4 all-gather.2
  381.8 75.8 reduce-scatter.4
  460.0 72.3 reduce-scatter.2
where the time goes:
time: 551 us; the launch traced here: 541 us
  waiting for transfers between devices  179 us (32%)
  local copies, waits for them, and re-layouts  128 us (23%)
  other arithmetic  108 us (20%)
  matrix products  58.7 us (11%)
  blocking collectives  43.3 us (8%)
  between operations  16.9 us (3%)
  starting transfers between devices  5.54 us (1%)
    reduce_scatter x1, waiting for transfers between devices, local(): lax.psum_scatter(numer, 'epoch', scatter_dimension=0, tiled=True)  74.7 us
    all_gather x1, waiting for transfers between devices, local(): basis = lax.all_gather(own, 'epoch', axis=1, tiled=True)  61.3 us
    gather x48, local copies, waits for them, and re-layouts  59 us
    all_gather x1, blocking collectives, local(): whole = lax.all_gather(template[0], 'epoch', axis=0, tiled=True)  43.3 us
    reduce_scatter x1, waiting for transfers between devices, local(): lax.psum_scatter(total, 'epoch', scatter_dimension=0, tiled=True)  40.8 us
    another operation x24, other arithmetic, fit_epoch(): factor = jnp.linalg.cholesky(system)  38.2 us
    unnamed x85, local copies, waits for them, and re-layouts  32.9 us
    another operation x16, other arithmetic, fit_epoch(): lax.linalg.triangular_solve(factor, first, left_side=True, lower=True, tr...  32.8 us
  transfers between devices with their start and end apart: 7, of which 5 were waited for; matrix products, arithmetic and copies ran while one was open for 8% of the time, Pallas kernels for 0%

commit v1 on v0

v1 whole, which is shorter than its diff:
```python
import functools

import jax
import jax.numpy as jnp
import ml_dtypes
import numpy as np
from jax import lax
from jax.experimental import pallas as pl
from jax.experimental.pallas import tpu as pltpu
from jax.sharding import PartitionSpec as P

NB = 45
NBP = 48
HALF = 11
SHIFT = 8
W = 128
H = 256
G = 16
WIN = 3 * G
SIGMAS = (0.75, 1.5, 3.0)
NF = 15
RIDGE = 0.5
SCI = 16
MESH = pl.DeviceIdType.MESH
VMEM = pl.BlockSpec(memory_space=pltpu.VMEM)
SMEM = pl.BlockSpec(memory_space=pltpu.SMEM)


def taps(offset, sigma, power):
    ratio = offset.astype(np.float64) / sigma
    values = ratio**power * np.exp(-0.5 * ratio * ratio)
    return np.where(np.abs(offset) <= HALF, values, 0.0)


def split(values):
    values = values.astype(np.float32)
    high = values.astype(ml_dtypes.bfloat16)
    low = (values - high.astype(np.float32)).astype(ml_dtypes.bfloat16)
    return high, low


def column_taps():
    spot = np.arange(W)
    source = np.concatenate([spot, np.where(spot < W // 2, spot + W, spot - W)])
    offset = spot[None, :] - source[:, None]
    return split(np.concatenate([taps(offset, s, p) for s in SIGMAS for p in range(5)], axis=1))


def row_taps():
    offset = np.arange(G)[:, None] + G - np.arange(WIN)[None, :]
    out = np.zeros((G, NBP, NF, WIN))
    b = 0
    for i, sigma in enumerate(SIGMAS):
        for p in range(5):
            for q in range(5 - p):
                out[:, b, i * 5 + p, :] = taps(offset, sigma, q)
                b += 1
    return split(out.reshape(G * NBP, NF * WIN))


def spreads(epochs):
    tile = np.zeros((NBP, G, NBP))
    tile[np.arange(NBP), :, np.arange(NBP)] = 1.0
    keep = np.zeros((epochs, G, G, NBP))
    keep[:, np.arange(G), np.arange(G), :] = 1.0
    return (
        tile.reshape(NBP, G * NBP).astype(ml_dtypes.bfloat16),
        keep.reshape(epochs * G, G * NBP).astype(np.float32),
    )


def greet(tiles, epochs, tile, me):
    barrier = pltpu.get_barrier_semaphore()

    def hello(step, carry):
        peer = lax.rem(me + step, epochs)
        pl.semaphore_signal(barrier, inc=1, device_id=(tile, peer), device_id_type=MESH)
        return carry

    lax.fori_loop(1, epochs, hello, 0)
    for step in (1, tiles - 1):
        near = lax.rem(tile + step, tiles)
        pl.semaphore_signal(barrier, inc=1, device_id=(near, me), device_id_type=MESH)
    pl.semaphore_wait(barrier, epochs + 1)


def gather_kernel(tiles, epochs, rows, mine, own, left, right, send, recv, side_send, side_recv, local):
    tile = lax.axis_index("tile")
    me = lax.axis_index("epoch")
    greet(tiles, epochs, tile, me)

    def band(which):
        return pl.ds(pl.multiple_of(which * rows, rows), rows)

    def copy(step):
        peer = lax.rem(me + step, epochs)
        return pltpu.make_async_remote_copy(
            src_ref=mine,
            dst_ref=own.at[band(me)],
            send_sem=send.at[step],
            recv_sem=recv.at[step],
            device_id=(tile, peer),
            device_id_type=MESH,
        )

    def start(step, carry):
        copy(step).start()
        return carry

    def finish(step, carry):
        copy(step).wait_recv()
        copy(step).wait_send()
        return carry

    lax.fori_loop(1, epochs, start, 0)
    here = pltpu.make_async_copy(mine, own.at[band(me)], local)
    here.start()
    here.wait()
    lax.fori_loop(1, epochs, finish, 0)
    sides = []
    for i, (step, target) in enumerate(((1, left), (tiles - 1, right))):
        side = pltpu.make_async_remote_copy(
            src_ref=own,
            dst_ref=target,
            send_sem=side_send.at[i],
            recv_sem=side_recv.at[i],
            device_id=(lax.rem(tile + step, tiles), me),
            device_id_type=MESH,
        )
        side.start()
        sides.append(side)
    for side in sides:
        side.wait()


def gather(mesh_sizes, template):
    tiles, epochs = mesh_sizes
    rows = template.shape[0]
    whole = jax.ShapeDtypeStruct((H, W), jnp.float32)
    return pl.pallas_call(
        functools.partial(gather_kernel, tiles, epochs, rows),
        out_shape=(whole, whole, whole),
        in_specs=[VMEM],
        out_specs=(VMEM, VMEM, VMEM),
        scratch_shapes=[
            pltpu.SemaphoreType.DMA((epochs,)),
            pltpu.SemaphoreType.DMA((epochs,)),
            pltpu.SemaphoreType.DMA((2,)),
            pltpu.SemaphoreType.DMA((2,)),
            pltpu.SemaphoreType.DMA,
        ],
        compiler_params=pltpu.CompilerParams(collective_id=0, has_side_effects=True),
        name="gather_template",
    )(template)


def dot(a, b):
    return jnp.dot(a, b, preferred_element_type=jnp.float32)


def halves(values):
    high = values.astype(jnp.bfloat16)
    return high, (values - high.astype(jnp.float32)).astype(jnp.bfloat16)


def fit_kernel(
    tiles, epochs,
    own, left, right, turned, science, weights, shifts, valid, counts, ch, cl, rh, rl, spread, keep,
    coef_out, sky_out, spill_out,
    fh, fl, basis, lhs, rhs, gram, moved,
):
    tile = lax.axis_index("tile")
    me = lax.axis_index("epoch")
    here = science.shape[0]

    mean = 1.0 / (H * W)
    lane = lax.broadcasted_iota(jnp.int32, (H, W), 1)
    mid = own[...] - jnp.sum(own[...]) * mean
    before = (left[...] - jnp.sum(left[...]) * mean) * (tile > 0).astype(jnp.float32)
    after = (right[...] - jnp.sum(right[...]) * mean) * (tile < tiles - 1).astype(jnp.float32)
    ref = jnp.concatenate([mid, jnp.where(lane < W // 2, after, before)], axis=1)
    high, low = halves(ref)
    zeros = jnp.zeros((NF, G, W), jnp.bfloat16)
    for buf in (fh, fl):
        buf[:, 0:G, :] = zeros
        buf[:, G + H : G + H + G, :] = zeros
    for f in range(NF):
        cols = slice(f * W, (f + 1) * W)
        out = dot(high, ch[:, cols]) + (dot(low, ch[:, cols]) + dot(high, cl[:, cols]))
        fhigh, flow = halves(out)
        fh[f, G : G + H, :] = fhigh
        fl[f, G : G + H, :] = flow

    gram[...] = jnp.zeros_like(gram)

    def block(i, carry):
        top = pl.multiple_of(i * G, G)
        wh = fh[:, pl.ds(top, WIN), :].reshape(NF * WIN, W)
        wl = fl[:, pl.ds(top, WIN), :].reshape(NF * WIN, W)
        both = dot(rh[...], jnp.concatenate([wh, wl], axis=1))
        values = both[:, :W] + (both[:, W:] + dot(rl[...], wh))
        values = values.astype(jnp.bfloat16)
        basis[pl.ds(pl.multiple_of(i * (G * NBP), G * NBP), G * NBP), :] = values
        for r in range(G):
            cols = slice(r * W, (r + 1) * W)
            part = values[r * NBP : (r + 1) * NBP, :]
            rhs[0:NBP, cols] = part
            rhs[NBP : NBP + SCI, cols] = turned[top + r]
            wide = part.astype(jnp.float32)
            for e in range(here):
                lhs[e * NBP : (e + 1) * NBP, cols] = (
                    wide * weights[e, pl.ds(top + r, 1), :]
                ).astype(jnp.bfloat16)
        gram[...] += lax.dot_general(
            lhs[...], rhs[...], (((1,), (1,)), ((), ())), preferred_element_type=jnp.float32
        )
        return carry

    lax.fori_loop(0, H // G, block, 0)

    wide = NBP + SCI
    eye = (
        lax.broadcasted_iota(jnp.int32, (NBP, NBP), 0)
        == lax.broadcasted_iota(jnp.int32, (NBP, NBP), 1)
    ).astype(jnp.float32)
    col = lax.broadcasted_iota(jnp.int32, (NBP, SCI), 1)
    systems = []
    scales = []
    for e in range(here):
        full = gram[e * NBP : (e + 1) * NBP, :]
        square = full[:, :NBP]
        square = 0.5 * (square + square.T)
        diag = square * eye
        down = lax.rsqrt(jnp.sum(diag, axis=1, keepdims=True) + 1e-06)
        across = lax.rsqrt(jnp.sum(diag, axis=0, keepdims=True) + 1e-06)
        proj = jnp.sum(jnp.where(col == e, full[:, NBP:], 0.0), axis=1, keepdims=True) * down
        square = square * (down * across) + RIDGE * eye
        systems.append(jnp.concatenate([square, jnp.where(col == 0, proj, 0.0)], axis=1))
        scales.append(across)
    a = jnp.stack(systems)
    row = lax.broadcasted_iota(jnp.int32, (here, NBP, 1), 1)
    for k in range(NB):
        pivot = a[:, k : k + 1, :]
        pivot = pivot * (1.0 / pivot[:, :, k : k + 1])
        factor = jnp.where(row == k, 0.0, a[:, :, k : k + 1])
        a = a - factor * pivot
    ys = []
    for e in range(here):
        diag = jnp.sum(a[e, :, :NBP] * eye, axis=1, keepdims=True)
        ys.append(jnp.sum((a[e, :, NBP : NBP + 1] / diag) * eye, axis=0, keepdims=True))
    lives = [
        (valid[0, e] * (me * here + e < counts[0]).astype(jnp.int32)).astype(jnp.float32)
        for e in range(here)
    ]
    coef_out[...] = jnp.concatenate([lives[e] * ys[e] for e in range(here)], axis=0)[:, :NB]
    ks = jnp.concatenate([ys[e] * scales[e] for e in range(here)], axis=0).astype(jnp.bfloat16)
    spun = dot(ks, spread[...])
    spun = jnp.broadcast_to(spun[:, None, :], (here, G, G * NBP)).reshape(here * G, G * NBP)
    mixer = (spun * keep[...]).astype(jnp.bfloat16)

    moved[:, :, 0:SHIFT, :] = jnp.zeros((here, 2, SHIFT, W), jnp.float32)
    moved[:, :, SHIFT + H :, :] = jnp.zeros((here, 2, SHIFT, W), jnp.float32)

    def differ(i, carry):
        top = pl.multiple_of(i * G, G)
        part = basis[pl.ds(pl.multiple_of(i * (G * NBP), G * NBP), G * NBP), :]
        model = dot(mixer, part)
        for e in range(here):
            diff = science[e, pl.ds(top, G), :].astype(jnp.float32) - model[e * G : (e + 1) * G, :]
            mass = lives[e] * weights[e, pl.ds(top, G), :]
            run = lax.rem(shifts[e, 1] + W, W)
            spot = pl.ds(pl.multiple_of(top + SHIFT, SHIFT), G)
            moved[e, 0, spot, :] = pltpu.roll(mass * diff, run, 1)
            moved[e, 1, spot, :] = pltpu.roll(mass, run, 1)
        return carry

    lax.fori_loop(0, H // G, differ, 0)

    bands, _, rows, _ = sky_out.shape
    for field in range(2):
        sky = jnp.zeros((H, W), jnp.float32)
        spill = jnp.zeros((H, W), jnp.float32)
        for e in range(here):
            values = moved[e, field, pl.ds(SHIFT - shifts[e, 0], H), :]
            source = lane - shifts[e, 1]
            inside = (source >= 0) & (source < W)
            sky += jnp.where(inside, values, 0.0)
            spill += jnp.where(inside, 0.0, values)
        sky_out[:, field] = sky.reshape(bands, rows, W)
        spill_out[:, field] = spill.reshape(bands, rows, W)


def fit(mesh_sizes, rows, own, left, right, turned, science, weights, shifts, valid, counts):
    tiles, epochs = mesh_sizes
    here = science.shape[0]
    ch, cl = column_taps()
    rh, rl = row_taps()
    spread, keep = spreads(here)
    sky = jax.ShapeDtypeStruct((epochs, 2, rows, W), jnp.float32)
    return pl.pallas_call(
        functools.partial(fit_kernel, tiles, epochs),
        out_shape=(jax.ShapeDtypeStruct((here, NB), jnp.float32), sky, sky),
        in_specs=[VMEM] * 6 + [SMEM] * 3 + [VMEM] * 6,
        out_specs=(VMEM, VMEM, VMEM),
        scratch_shapes=[
            pltpu.VMEM((NF, H + 2 * G, W), jnp.bfloat16),
            pltpu.VMEM((NF, H + 2 * G, W), jnp.bfloat16),
            pltpu.VMEM((H * NBP, W), jnp.bfloat16),
            pltpu.VMEM((here * NBP, G * W), jnp.bfloat16),
            pltpu.VMEM((NBP + SCI, G * W), jnp.bfloat16),
            pltpu.VMEM((here * NBP, NBP + SCI), jnp.float32),
            pltpu.VMEM((here, 2, H + 2 * SHIFT, W), jnp.float32),
        ],
        compiler_params=pltpu.CompilerParams(vmem_limit_bytes=48 * 1024 * 1024),
        name="fit_epochs",
    )(own, left, right, turned, science, weights, shifts, valid, counts, ch, cl, rh, rl, spread, keep)


def coadd_kernel(
    tiles, epochs, sky, spill, out, whole, from_left, from_right, parts, send, recv, side_send, side_recv
):
    tile = lax.axis_index("tile")
    me = lax.axis_index("epoch")
    greet(tiles, epochs, tile, me)
    sides = []
    for i, (step, target) in enumerate(((1, from_left), (tiles - 1, from_right))):
        side = pltpu.make_async_remote_copy(
            src_ref=spill,
            dst_ref=target,
            send_sem=side_send.at[i],
            recv_sem=side_recv.at[i],
            device_id=(lax.rem(tile + step, tiles), me),
            device_id_type=MESH,
        )
        side.start()
        sides.append(side)
    for side in sides:
        side.wait()
    lane = lax.broadcasted_iota(jnp.int32, sky.shape, 3)
    has_left = (tile > 0).astype(jnp.float32)
    has_right = (tile < tiles - 1).astype(jnp.float32)
    whole[...] = sky[...] + (
        jnp.where(lane < SHIFT, from_left[...], 0.0) * has_left
        + jnp.where(lane >= W - SHIFT, from_right[...], 0.0) * has_right
    )

    def copy(step):
        peer = lax.rem(me + step, epochs)
        return pltpu.make_async_remote_copy(
            src_ref=whole.at[peer],
            dst_ref=parts.at[step],
            send_sem=send.at[step],
            recv_sem=recv.at[step],
            device_id=(tile, peer),
            device_id_type=MESH,
        )

    def start(step, carry):
        copy(step).start()
        return carry

    def finish(step, total):
        copy(step).wait_recv()
        copy(step).wait_send()
        return total + parts[step]

    lax.fori_loop(1, epochs, start, 0)
    total = lax.fori_loop(1, epochs, finish, whole[me])
    out[...] = total[0] / jnp.sqrt(1.0 + total[1])


def coadd(mesh_sizes, sky, spill):
    tiles, epochs = mesh_sizes
    rows = sky.shape[2]
    return pl.pallas_call(
        functools.partial(coadd_kernel, tiles, epochs),
        out_shape=jax.ShapeDtypeStruct((rows, W), jnp.float32),
        in_specs=[VMEM, VMEM],
        out_specs=VMEM,
        scratch_shapes=[
            pltpu.VMEM(sky.shape, jnp.float32),
            pltpu.VMEM(sky.shape, jnp.float32),
            pltpu.VMEM(sky.shape, jnp.float32),
            pltpu.VMEM(sky.shape, jnp.float32),
            pltpu.SemaphoreType.DMA((epochs,)),
            pltpu.SemaphoreType.DMA((epochs,)),
            pltpu.SemaphoreType.DMA((2,)),
            pltpu.SemaphoreType.DMA((2,)),
        ],
        compiler_params=pltpu.CompilerParams(collective_id=1, has_side_effects=True),
        name="coadd_bands",
    )(sky, spill)


def local(mesh_sizes, template, science, weights, shifts, valid, counts):
    here = science.shape[1]
    turned = jnp.transpose(science[0], (1, 0, 2))
    turned = jnp.pad(turned, ((0, 0), (0, SCI - here), (0, 0)))
    own, left, right = gather(mesh_sizes, template[0])
    coefs, sky, spill = fit(
        mesh_sizes, template.shape[1], own, left, right, turned, science[0], weights[0], shifts, valid, counts
    )
    return (coadd(mesh_sizes, sky, spill)[None], coefs[None])


def solution(mesh):
    sizes = (mesh.shape["tile"], mesh.shape["epoch"])
    in_specs = (
        P("tile", "epoch", None),
        P("tile", "epoch", None, None),
        P("tile", "epoch", None, None),
        P("epoch", None),
        P("tile", "epoch"),
        P("tile"),
    )
    out_specs = (P("tile", "epoch", None), P("tile", "epoch", None))
    return jax.shard_map(
        functools.partial(local, sizes), mesh=mesh, in_specs=in_specs, out_specs=out_specs, check_vma=False
    )
```

time: 551 us -> 75 us (0.14); the launches traced: 541 us -> 74.5 us
  waiting for transfers between devices: 179 us -> 0 us
  local copies, waits for them, and re-layouts: 128 us -> 10.1 us
  other arithmetic: 108 us -> 0 us
  Pallas kernels: 0 us -> 63 us
  matrix products: 58.7 us -> 0 us
  blocking collectives: 43.3 us -> 0 us
  between operations: 16.9 us -> 1.41 us
  starting transfers between devices: 5.54 us -> 0 us
    reduce_scatter x2 -> x0, waiting for transfers between devices: 115 us -> none  [the longest x1 74.7 us: local(): lax.psum_scatter(numer, 'epoch', scatter_dimension=0, tiled=True)]
    gather x56 -> x0, local copies, waits for them, and re-layouts: 75.5 us -> none
    another operation x43 -> x0, other arithmetic: 75.1 us -> none  [the longest x24 38.2 us: fit_epoch(): factor = jnp.linalg.cholesky(system)]
    pallas_call x0 -> x3, Pallas kernels: none -> 63 us  [the longest x1 35.9 us: fit(): pl.pallas_call(functools.partial(fit_kernel, tiles, epochs), out_shape=(j...]
    all_gather x1 -> x0, waiting for transfers between devices: 61.3 us -> none  [local(): basis = lax.all_gather(own, 'epoch', axis=1, tiled=True)]
    dot_general x84 -> x0, matrix products: 56.3 us -> none  [the longest x8 27.6 us: fit_epoch(): lax.dot_general(weighted, basis, (((1,), (1,)), ((), ())), preferred_elem...]
    all_gather x1 -> x0, blocking collectives: 43.3 us -> none  [local(): whole = lax.all_gather(template[0], 'epoch', axis=0, tiled=True)]
    unnamed x85 -> x27, local copies, waits for them, and re-layouts: 32.9 us -> 9.99 us
  transfers between devices with their start and end apart: 7 -> 0, of which waited for: 5 -> 0; matrix products, arithmetic and copies ran while one was open for 8% -> 0% of each run, Pallas kernels for 0% -> 0%
where the time goes in v1:
time: 75 us; the launch traced here: 74.5 us
  Pallas kernels  63 us (84%)
  local copies, waits for them, and re-layouts  10.1 us (13%)
  between operations  1.41 us (2%)
    pallas_call x1, Pallas kernels, fit(): pl.pallas_call(functools.partial(fit_kernel, tiles, epochs), out_shape=(j...  35.9 us
    pallas_call x1, Pallas kernels, coadd(): pl.pallas_call(functools.partial(coadd_kernel, tiles, epochs), out_shape=...  14.1 us
    pallas_call x1, Pallas kernels, gather(): pl.pallas_call(functools.partial(gather_kernel, tiles, epochs, rows), out...  12.9 us
    unnamed x27, local copies, waits for them, and re-layouts  9.99 us

profile of v1, /device:TPU:0, one launch (start us, length us, event | category | flops | bytes accessed | tf_op | source)
XLA Modules:
  0.0 74.5 jit_solution(6426028869574159983)
XLA Ops:
  0.6 0.0 copy-start.10
  1.3 0.8 %copy.15.shifts = s32[8,2]{1,0:T(8,128)S(1)} copy(s32[8,2]{0,1:T(2,128)} %param.15) | data formatting | bytes 128 | tf_op args[3]
  2.1 12.9 %gather_template.1 = (f32[256,128]{1,0:T(8,128)}, f32[256,128]{1,0:T(8,128)}, f32[256,128]{1,0:T(8,128)}) custom-call(f32[16,128]{1,0:T(8,128)} %bitcast.11), custom_call_target="tpu_custom_call" | custom-call | tf_op jit(solution)/shard_map/gather_template/pallas_call | solution.py:140
  15.0 0.0 copy-start
  15.0 0.0 copy-start.1
  15.0 0.0 copy-start.2
  15.0 0.0 copy-start.11
  15.0 1.5 %copy.16 = bf16[256,8,128]{2,1,0:T(8,128)(2,1)S(1)} copy(bf16[256,8,128]{2,0,1:T(8,128)(2,1)} %bitcast.7) | data formatting | bytes 1048576
  16.6 0.1 pad.4.clone.turned
  16.7 0.0 copy-done.10
  16.8 0.0 copy-done
  16.8 0.0 copy-done.1
  16.8 0.1 copy-done.2
  16.8 0.0 copy-done.11
  16.8 0.0 copy-start.3
  16.8 1.2 %copy-done.3 = bf16[256,1920]{1,0:T(8,128)(2,1)S(1)} copy-done((bf16[256,1920]{1,0:T(8,128)(2,1)S(1)}, bf16[256,1920]{1,0:T(8,128)(2,1)}, u32[]{:S(2)}) %copy-start.3) | copy-done | bytes 983064
  18.1 0.0 copy-start.4
  18.1 1.0 %copy-done.4 = f32[128,768]{1,0:T(8,128)S(1)} copy-done((f32[128,768]{1,0:T(8,128)S(1)}, f32[128,768]{1,0:T(8,128)}, u32[]{:S(2)}) %copy-start.4) | copy-done | bytes 393240
  19.0 0.0 copy-start.7
  19.0 0.9 %copy-done.7 = f32[256,128]{1,0:T(8,128)S(1)} copy-done((f32[256,128]{1,0:T(8,128)S(1)}, f32[256,128]{1,0:T(8,128)}, u32[]{:S(2)}) %copy-start.7) | copy-done | bytes 131096
  20.0 0.0 copy-start.8
  20.0 0.9 %copy-done.8 = f32[256,128]{1,0:T(8,128)S(1)} copy-done((f32[256,128]{1,0:T(8,128)S(1)}, f32[256,128]{1,0:T(8,128)}, u32[]{:S(2)}) %copy-start.8) | copy-done | bytes 131096
  20.9 0.0 copy-start.9
  20.9 0.9 %copy-done.9 = f32[256,128]{1,0:T(8,128)S(1)} copy-done((f32[256,128]{1,0:T(8,128)S(1)}, f32[256,128]{1,0:T(8,128)}, u32[]{:S(2)}) %copy-start.9) | copy-done | bytes 131096
  21.8 35.9 %fit_epochs.1 = (f32[8,45]{1,0:T(8,128)}, f32[16,2,16,128]{3,2,1,0:T(8,128)S(1)}, f32[16,2,16,128]{3,2,1,0:T(8,128)S(1)}) custom-call(f32[256,128]{1,0:T(8,128)S(1)} %copy-done.7, f32[256,128]{1,0:T(8,128)S(1)} %copy-done.8, f32[256,128]{1,0:T(8,128)S(1)} %copy-done.9, bf16[256,16,128]{2,1,0:T(8,128)(2,1)S(1)} %pad.4.clone.turned, ...), custom_call_target="tpu_custom_call" | custom-call | tf_op jit(solution)/shard_map/fit_epochs/pallas_call | solution.py:300
  57.7 0.0 copy-start.5
  57.7 0.7 copy-done.5
  58.4 0.0 copy-start.6
  58.4 0.7 copy-done.6
  59.1 14.1 %coadd_bands.1 = f32[16,128]{1,0:T(8,128)} custom-call(f32[16,2,16,128]{3,2,1,0:T(8,128)} %copy-done.5, f32[16,2,16,128]{3,2,1,0:T(8,128)} %copy-done.6), custom_call_target="tpu_custom_call" | custom-call | tf_op jit(solution)/shard_map/coadd_bands/pallas_call | solution.py:375
  73.2 1.3 %copy.19 = f32[1,16,128]{2,1,0:T(8,128)} copy(f32[1,16,128]{2,1,0:T(8,128)} %bitcast.10) | data formatting | bytes 16384
Async XLA Ops:
  0.6 16.1 %copy-start.10 = (bf16[48,768]{1,0:T(8,128)(2,1)S(1)}, bf16[48,768]{1,0:T(8,128)(2,1)}, u32[]{:S(2)}) copy-start(bf16[48,768]{1,0:T(8,128)(2,1)} %constant.19.clone.spread) | copy-start | bytes 221188
  15.0 1.8 %copy-start = (bf16[1,8,256,128]{3,2,1,0:T(8,128)(2,1)S(1)}, bf16[1,8,256,128]{3,2,1,0:T(8,128)(2,1)}, u32[]{:S(2)}) copy-start(bf16[1,8,256,128]{3,2,1,0:T(8,128)(2,1)} %param.13) | copy-start | bytes 1572868
  15.0 1.8 %copy-start.1 = (f32[1,8,256,128]{3,2,1,0:T(8,128)S(1)}, f32[1,8,256,128]{3,2,1,0:T(8,128)}, u32[]{:S(2)}) copy-start(f32[1,8,256,128]{3,2,1,0:T(8,128)} %param.14) | copy-start | bytes 3145732
  15.0 1.8 %copy-start.2 = (bf16[256,1920]{1,0:T(8,128)(2,1)S(1)}, bf16[256,1920]{1,0:T(8,128)(2,1)}, u32[]{:S(2)}) copy-start(bf16[256,1920]{1,0:T(8,128)(2,1)} %constant.16.clone.cl) | copy-start | bytes 2949124
  15.0 1.8 %copy-start.11 = (s32[1,8]{1,0:T(1,128)S(1)}, s32[1,8]{1,0:T(1,128)}, u32[]{:S(2)}) copy-start(s32[1,8]{1,0:T(1,128)} %valid.1) | copy-start | bytes 100
  16.8 1.2 %copy-start.3 = (bf16[256,1920]{1,0:T(8,128)(2,1)S(1)}, bf16[256,1920]{1,0:T(8,128)(2,1)}, u32[]{:S(2)}) copy-start(bf16[256,1920]{1,0:T(8,128)(2,1)} %constant.15.clone.ch) | copy-start | bytes 2949124
  18.1 1.0 %copy-start.4 = (f32[128,768]{1,0:T(8,128)S(1)}, f32[128,768]{1,0:T(8,128)}, u32[]{:S(2)}) copy-start(f32[128,768]{1,0:T(8,128)} %constant.20.clone.keep) | copy-start | bytes 1179652
  19.0 0.9 %copy-start.7 = (f32[256,128]{1,0:T(8,128)S(1)}, f32[256,128]{1,0:T(8,128)}, u32[]{:S(2)}) copy-start(f32[256,128]{1,0:T(8,128)} %get-tuple-element.8.own) | copy-start | bytes 393220
  20.0 0.9 %copy-start.8 = (f32[256,128]{1,0:T(8,128)S(1)}, f32[256,128]{1,0:T(8,128)}, u32[]{:S(2)}) copy-start(f32[256,128]{1,0:T(8,128)} %get-tuple-element.9.left) | copy-start | bytes 393220
  20.9 0.9 %copy-start.9 = (f32[256,128]{1,0:T(8,128)S(1)}, f32[256,128]{1,0:T(8,128)}, u32[]{:S(2)}) copy-start(f32[256,128]{1,0:T(8,128)} %get-tuple-element.10.right) | copy-start | bytes 393220
  57.7 0.7 copy-start.5
  58.4 0.7 copy-start.6

commit v2 on v0

v2 whole, which is shorter than its diff:
```python
import functools

import jax
import jax.numpy as jnp
import numpy as np
from jax import lax
from jax.experimental import pallas as pl
from jax.experimental.pallas import tpu as pltpu
from jax.sharding import PartitionSpec as P

NB = 45
PER = 16
HALF = 11
SHIFT = 8
W = 128
H = 256
G = 16
WIN = 3 * G
SIGMAS = (0.75, 1.5, 3.0)
NF = 15
NS = 3
NBP = NS * PER
RIDGE = 0.5
SCI = 16
MESH = pl.DeviceIdType.MESH
VMEM = pl.BlockSpec(memory_space=pltpu.VMEM)
SMEM = pl.BlockSpec(memory_space=pltpu.SMEM)
HBM = pl.BlockSpec(memory_space=pltpu.HBM)


def taps(offset, sigma, power):
    ratio = offset.astype(np.float64) / sigma
    values = ratio**power * np.exp(-0.5 * ratio * ratio)
    return np.where(np.abs(offset) <= HALF, values, 0.0)


def column_taps():
    spot = np.arange(W)
    source = np.concatenate([spot, np.where(spot < W // 2, spot + W, spot - W)])
    offset = spot[None, :] - source[:, None]
    return np.concatenate([taps(offset, s, p) for s in SIGMAS for p in range(5)], axis=1).astype(np.float32)


def row_taps():
    offset = np.arange(G)[:, None] + G - np.arange(WIN)[None, :]
    out = np.zeros((NS, G, PER, 5, WIN))
    for i, sigma in enumerate(SIGMAS):
        for b, (p, q) in enumerate((p, q) for p in range(5) for q in range(5 - p)):
            out[i, :, b, p, :] = taps(offset, sigma, q)
    return out.reshape(NS, G * PER, 5 * WIN).astype(np.float32)


def greet(tiles, epochs, tile, me):
    barrier = pltpu.get_barrier_semaphore()

    def hello(step, carry):
        peer = lax.rem(me + step, epochs)
        pl.semaphore_signal(barrier, inc=1, device_id=(tile, peer), device_id_type=MESH)
        return carry

    lax.fori_loop(1, epochs, hello, 0)
    for step in (1, tiles - 1):
        near = lax.rem(tile + step, tiles)
        pl.semaphore_signal(barrier, inc=1, device_id=(near, me), device_id_type=MESH)
    pl.semaphore_wait(barrier, epochs + 1)


def dot(a, b):
    return jnp.dot(a, b, preferred_element_type=jnp.float32)


def halves(values):
    high = values.astype(jnp.bfloat16)
    return high, (values - high.astype(jnp.float32)).astype(jnp.bfloat16)


def iota(shape, axis):
    return lax.broadcasted_iota(jnp.int32, shape, axis)


def kernel(
    tiles, epochs,
    template, science_hbm, weights_hbm, shifts, valid, counts, col_hbm, row_hbm,
    coadd_out, coef_out,
    science, weights, col_wide, row_wide, ch, cl, rh, rl,
    own, left, right, fh, fl, basis, lhs, rhs, gram, moved, whole, spill, from_left, from_right, parts,
    load, send, recv, side_send, side_recv,
):
    tile = lax.axis_index("tile")
    me = lax.axis_index("epoch")
    here = science.shape[0]
    bands, rows = whole.shape[1], whole.shape[2]
    lane = iota((H, W), 1)
    has_left = (tile > 0).astype(jnp.float32)
    has_right = (tile < tiles - 1).astype(jnp.float32)

    loads = [
        pltpu.make_async_copy(src, dst, load.at[i])
        for i, (src, dst) in enumerate(
            ((weights_hbm, weights), (col_hbm, col_wide), (row_hbm, row_wide), (science_hbm, science))
        )
    ]
    for one in loads:
        one.start()
    greet(tiles, epochs, tile, me)

    def to_peers(kind, source, target):
        def copy(step):
            return pltpu.make_async_remote_copy(
                src_ref=source(lax.rem(me + step, epochs)),
                dst_ref=target(step),
                send_sem=send.at[kind, step],
                recv_sem=recv.at[kind, step],
                device_id=(tile, lax.rem(me + step, epochs)),
                device_id_type=MESH,
            )

        def start(step, carry):
            copy(step).start()
            return carry

        def finish(step, carry):
            copy(step).wait_recv()
            copy(step).wait_send()
            return carry

        lax.fori_loop(1, epochs, start, 0)
        return lambda: lax.fori_loop(1, epochs, finish, 0)

    def to_sides(kind, source, to_right, to_left):
        sides = [
            pltpu.make_async_remote_copy(
                src_ref=source,
                dst_ref=target,
                send_sem=side_send.at[kind, i],
                recv_sem=side_recv.at[kind, i],
                device_id=(lax.rem(tile + step, tiles), me),
                device_id_type=MESH,
            )
            for i, (step, target) in enumerate(((1, to_right), (tiles - 1, to_left)))
        ]
        for side in sides:
            side.start()

        def finish():
            for side in sides:
                side.wait()

        return finish

    band = pl.ds(pl.multiple_of(me * rows, rows), rows)
    template_done = to_peers(0, lambda peer: template, lambda step: own.at[band])
    own[band, :] = template[...]

    lives = [
        (valid[0, e] * (me * here + e < counts[0]).astype(jnp.int32)).astype(jnp.float32)
        for e in range(here)
    ]
    runs = [lax.rem(shifts[e, 1] + W, W) for e in range(here)]

    def gather_sky(field):
        sky = jnp.zeros((H, W), jnp.float32)
        over = jnp.zeros((H, W), jnp.float32)
        for e in range(here):
            values = moved[e, pl.ds(SHIFT - shifts[e, 0], H), :]
            origin = lane - shifts[e, 1]
            inside = (origin >= 0) & (origin < W)
            sky += jnp.where(inside, values, 0.0)
            over += jnp.where(inside, 0.0, values)
        whole[field] = sky.reshape(bands, rows, W)
        spill[field] = over.reshape(bands, rows, W)
        return to_sides(1 + field, spill.at[field], from_left.at[field], from_right.at[field])

    def merge(field):
        spot = iota((bands, rows, W), 2)
        whole[field] = whole[field] + (
            jnp.where(spot < SHIFT, from_left[field], 0.0) * has_left
            + jnp.where(spot >= W - SHIFT, from_right[field], 0.0) * has_right
        )
        return to_peers(
            1 + field, lambda peer: whole.at[field, peer], lambda step: parts.at[field, step]
        )

    def total_of(field):
        def add(step, total):
            return total + parts[field, step]

        return lax.fori_loop(1, epochs, add, whole[field, me])

    moved[:, 0:SHIFT, :] = jnp.zeros((here, SHIFT, W), jnp.float32)
    moved[:, SHIFT + H :, :] = jnp.zeros((here, SHIFT, W), jnp.float32)
    loads[0].wait()
    for e in range(here):
        moved[e, SHIFT : SHIFT + H, :] = pltpu.roll(lives[e] * weights[e], runs[e], 1)
    mass_sides = gather_sky(0)

    template_done()
    tile_sides = to_sides(0, own, left, right)
    mass_sides()
    mass_done = merge(0)

    loads[1].wait()
    ch[...], cl[...] = halves(col_wide[...])
    loads[2].wait()
    rh[...], rl[...] = halves(row_wide[...])
    zeros = jnp.zeros((NF, G, W), jnp.bfloat16)
    for buf in (fh, fl):
        buf[:, 0:G, :] = zeros
        buf[:, G + H : G + H + G, :] = zeros
    gram[...] = jnp.zeros_like(gram)
    tile_sides()

    mean = 1.0 / (H * W)
    mid = own[...] - jnp.sum(own[...]) * mean
    before = (left[...] - jnp.sum(left[...]) * mean) * has_left
    after = (right[...] - jnp.sum(right[...]) * mean) * has_right
    high, low = halves(jnp.concatenate([mid, jnp.where(lane < W // 2, after, before)], axis=1))
    for f in range(NF):
        cols = slice(f * W, (f + 1) * W)
        out = dot(high, ch[:, cols]) + (dot(low, ch[:, cols]) + dot(high, cl[:, cols]))
        fhigh, flow = halves(out)
        fh[f, G : G + H, :] = fhigh
        fl[f, G : G + H, :] = flow

    loads[3].wait()
    turn_to = iota((G * SCI, here * G), 0)
    turn_from = iota((G * SCI, here * G), 1)
    turn = (
        (turn_to // SCI == turn_from % G) & (turn_to % SCI == turn_from // G)
    ).astype(jnp.float32).astype(jnp.bfloat16)

    def block(i, carry):
        top = pl.multiple_of(i * G, G)
        pieces = []
        for s in range(NS):
            wh = fh[5 * s : 5 * s + 5, pl.ds(top, WIN), :].reshape(5 * WIN, W)
            wl = fl[5 * s : 5 * s + 5, pl.ds(top, WIN), :].reshape(5 * WIN, W)
            both = dot(rh[s], jnp.concatenate([wh, wl], axis=1))
            values = both[:, :W] + (both[:, W:] + dot(rl[s], wh))
            pieces.append(values.astype(jnp.bfloat16))
            first = pl.multiple_of(i * (G * NBP) + s * (G * PER), G * PER)
            basis[pl.ds(first, G * PER), :] = pieces[s]
        images = science[:, pl.ds(top, G), :].reshape(here * G, W)
        turned = dot(turn, images).astype(jnp.bfloat16)
        for r in range(G):
            cols = slice(r * W, (r + 1) * W)
            part = jnp.concatenate([piece[r * PER : (r + 1) * PER, :] for piece in pieces], axis=0)
            rhs[0:NBP, cols] = part
            rhs[NBP : NBP + SCI, cols] = turned[r * SCI : (r + 1) * SCI, :]
            wide = part.astype(jnp.float32)
            for e in range(here):
                lhs[e * NBP : (e + 1) * NBP, cols] = (
                    wide * weights[e, pl.ds(top + r, 1), :]
                ).astype(jnp.bfloat16)
        gram[...] += lax.dot_general(
            lhs[...], rhs[...], (((1,), (1,)), ((), ())), preferred_element_type=jnp.float32
        )
        return carry

    lax.fori_loop(0, H // G, block, 0)

    eye = (iota((NBP, NBP), 0) == iota((NBP, NBP), 1)).astype(jnp.float32)
    col = iota((NBP, SCI), 1)
    systems = []
    scales = []
    for e in range(here):
        full = gram[e * NBP : (e + 1) * NBP, :]
        square = full[:, :NBP]
        square = 0.5 * (square + square.T)
        diag = square * eye
        down = lax.rsqrt(jnp.sum(diag, axis=1, keepdims=True) + 1e-06)
        across = lax.rsqrt(jnp.sum(diag, axis=0, keepdims=True) + 1e-06)
        proj = jnp.sum(jnp.where(col == e, full[:, NBP:], 0.0), axis=1, keepdims=True) * down
        square = square * (down * across) + RIDGE * eye
        systems.append(jnp.concatenate([square, jnp.where(col == 0, proj, 0.0)], axis=1))
        scales.append(across)
    a = jnp.stack(systems)
    row = iota((here, NBP, 1), 1)
    for k in range(0, NBP, 2):
        r0, r1 = a[:, k : k + 1, :], a[:, k + 1 : k + 2, :]
        c0, c1 = a[:, :, k : k + 1], a[:, :, k + 1 : k + 2]
        p00, p01 = r0[:, :, k : k + 1], r0[:, :, k + 1 : k + 2]
        p10, p11 = r1[:, :, k : k + 1], r1[:, :, k + 1 : k + 2]
        inverse = 1.0 / (p00 * p11 - p01 * p10)
        q0 = (p11 * inverse) * r0 - (p01 * inverse) * r1
        q1 = (p00 * inverse) * r1 - (p10 * inverse) * r0
        a = a - (c0 - (row == k).astype(jnp.float32)) * q0 - (c1 - (row == k + 1).astype(jnp.float32)) * q1
    ys = [jnp.sum(a[e, :, NBP : NBP + 1] * eye, axis=0, keepdims=True) for e in range(here)]
    coefs = jnp.concatenate([lives[e] * ys[e] for e in range(here)], axis=0)
    coef_out[...] = jnp.concatenate(
        [coefs[:, s * PER : (s + 1) * PER - 1] for s in range(NS)], axis=1
    )
    ks = jnp.concatenate([ys[e] * scales[e] for e in range(here)], axis=0).astype(jnp.bfloat16)
    lanes = iota((NBP, G * NBP), 1)
    spread = (lanes // (G * PER) * PER + lanes % PER == iota((NBP, G * NBP), 0)).astype(jnp.float32).astype(jnp.bfloat16)
    spun = dot(ks, spread)
    spun = jnp.broadcast_to(spun[:, None, :], (here, G, G * NBP)).reshape(here * G, G * NBP)
    keep = iota((here * G, G * NBP), 0) % G == iota((here * G, G * NBP), 1) // PER % G
    mixer = jnp.where(keep, spun, 0.0).astype(jnp.bfloat16)

    def differ(i, carry):
        pair = [
            basis[pl.ds(pl.multiple_of((2 * i + j) * (G * NBP), G * NBP), G * NBP), :] for j in range(2)
        ]
        model = dot(mixer, jnp.concatenate(pair, axis=1))
        for j in range(2):
            top = pl.multiple_of((2 * i + j) * G, G)
            spot = pl.ds(pl.multiple_of(top + SHIFT, SHIFT), G)
            for e in range(here):
                fitted = model[e * G : (e + 1) * G, j * W : (j + 1) * W]
                diff = science[e, pl.ds(top, G), :].astype(jnp.float32) - fitted
                mass = lives[e] * weights[e, pl.ds(top, G), :]
                moved[e, spot, :] = pltpu.roll(mass * diff, runs[e], 1)
        return carry

    lax.fori_loop(0, H // G // 2, differ, 0)

    prod_sides = gather_sky(1)
    mass_done()
    total = total_of(0)
    prod_sides()
    prod_done = merge(1)
    root = lax.rsqrt(1.0 + total)
    prod_done()
    coadd_out[...] = total_of(1) * root


def local(mesh_sizes, template, science, weights, shifts, valid, counts):
    tiles, epochs = mesh_sizes
    rows = template.shape[1]
    here = science.shape[1]
    field = pltpu.VMEM((2, epochs, rows, W), jnp.float32)
    tile = pltpu.VMEM((H, W), jnp.float32)
    cols = column_taps()
    bands = row_taps()
    coadd, coefs = pl.pallas_call(
        functools.partial(kernel, tiles, epochs),
        out_shape=(
            jax.ShapeDtypeStruct((rows, W), jnp.float32),
            jax.ShapeDtypeStruct((here, NB), jnp.float32),
        ),
        in_specs=[VMEM, HBM, HBM, SMEM, SMEM, SMEM, HBM, HBM],
        out_specs=(VMEM, VMEM),
        scratch_shapes=[
            pltpu.VMEM((here, H, W), jnp.bfloat16),
            pltpu.VMEM((here, H, W), jnp.float32),
            pltpu.VMEM(cols.shape, jnp.float32),
            pltpu.VMEM(bands.shape, jnp.float32),
            pltpu.VMEM(cols.shape, jnp.bfloat16),
            pltpu.VMEM(cols.shape, jnp.bfloat16),
            pltpu.VMEM(bands.shape, jnp.bfloat16),
            pltpu.VMEM(bands.shape, jnp.bfloat16),
            tile,
            tile,
            tile,
            pltpu.VMEM((NF, H + 2 * G, W), jnp.bfloat16),
            pltpu.VMEM((NF, H + 2 * G, W), jnp.bfloat16),
            pltpu.VMEM((H * NBP, W), jnp.bfloat16),
            pltpu.VMEM((here * NBP, G * W), jnp.bfloat16),
            pltpu.VMEM((NBP + SCI, G * W), jnp.bfloat16),
            pltpu.VMEM((here * NBP, NBP + SCI), jnp.float32),
            pltpu.VMEM((here, H + 2 * SHIFT, W), jnp.float32),
            field,
            field,
            field,
            field,
            field,
            pltpu.SemaphoreType.DMA((4,)),
            pltpu.SemaphoreType.DMA((3, epochs)),
            pltpu.SemaphoreType.DMA((3, epochs)),
            pltpu.SemaphoreType.DMA((3, 2)),
            pltpu.SemaphoreType.DMA((3, 2)),
        ],
        compiler_params=pltpu.CompilerParams(
            collective_id=0, has_side_effects=True, vmem_limit_bytes=60 * 1024 * 1024
        ),
        name="difference_coadd",
    )(template[0], science[0], weights[0], shifts, valid, counts, cols, bands)
    return (coadd[None], coefs[None])


def solution(mesh):
    sizes = (mesh.shape["tile"], mesh.shape["epoch"])
    in_specs = (
        P("tile", "epoch", None),
        P("tile", "epoch", None, None),
        P("tile", "epoch", None, None),
        P("epoch", None),
        P("tile", "epoch"),
        P("tile"),
    )
    out_specs = (P("tile", "epoch", None), P("tile", "epoch", None))
    return jax.shard_map(
        functools.partial(local, sizes), mesh=mesh, in_specs=in_specs, out_specs=out_specs, check_vma=False
    )
```

time: 551 us -> 59.6 us (0.11); the launches traced: 541 us -> 59.2 us
  waiting for transfers between devices: 179 us -> 0 us
  local copies, waits for them, and re-layouts: 128 us -> 3.91 us
  other arithmetic: 108 us -> 0 us
  matrix products: 58.7 us -> 0 us
  Pallas kernels: 0 us -> 54.1 us
  blocking collectives: 43.3 us -> 0 us
  between operations: 16.9 us -> 1.29 us
  starting transfers between devices: 5.54 us -> 0 us
    reduce_scatter x2 -> x0, waiting for transfers between devices: 115 us -> none  [the longest x1 74.7 us: local(): lax.psum_scatter(numer, 'epoch', scatter_dimension=0, tiled=True)]
    gather x56 -> x0, local copies, waits for them, and re-layouts: 75.5 us -> none
    another operation x43 -> x0, other arithmetic: 75.1 us -> none  [the longest x24 38.2 us: fit_epoch(): factor = jnp.linalg.cholesky(system)]
    all_gather x1 -> x0, waiting for transfers between devices: 61.3 us -> none  [local(): basis = lax.all_gather(own, 'epoch', axis=1, tiled=True)]
    dot_general x84 -> x0, matrix products: 56.3 us -> none  [the longest x8 27.6 us: fit_epoch(): lax.dot_general(weighted, basis, (((1,), (1,)), ((), ())), preferred_elem...]
    pallas_call x0 -> x1, Pallas kernels: none -> 54.1 us  [local(): pl.pallas_call(functools.partial(kernel, tiles, epochs), out_shape=(jax.S...]
    all_gather x1 -> x0, blocking collectives: 43.3 us -> none  [local(): whole = lax.all_gather(template[0], 'epoch', axis=0, tiled=True)]
    unnamed x85 -> x3, local copies, waits for them, and re-layouts: 32.9 us -> 3.91 us
  transfers between devices with their start and end apart: 7 -> 0, of which waited for: 5 -> 0; matrix products, arithmetic and copies ran while one was open for 8% -> 0% of each run, Pallas kernels for 0% -> 0%
where the time goes in v2:
time: 59.6 us; the launch traced here: 59.2 us
  Pallas kernels  54.1 us (91%)
  local copies, waits for them, and re-layouts  3.91 us (7%)
  between operations  1.29 us (2%)
    pallas_call x1, Pallas kernels, local(): pl.pallas_call(functools.partial(kernel, tiles, epochs), out_shape=(jax.S...  54.1 us
    unnamed x3, local copies, waits for them, and re-layouts  3.91 us

profile of v2, /device:TPU:0, one launch (start us, length us, event | category | flops | bytes accessed | tf_op | source)
XLA Modules:
  0.0 59.2 jit_solution(9218072589977255848)
XLA Ops:
  1.3 1.3 %copy.10.shifts = s32[8,2]{1,0:T(8,128)} copy(s32[8,2]{0,1:T(2,128)} %param.11) | data formatting | bytes 128 | tf_op args[3]
  2.6 54.1 %difference_coadd.1 = (f32[16,128]{1,0:T(8,128)}, f32[8,45]{1,0:T(8,128)}) custom-call(f32[16,128]{1,0:T(8,128)} %bitcast.7, bf16[8,256,128]{2,1,0:T(8,128)(2,1)} %bitcast.6, f32[8,256,128]{2,1,0:T(8,128)} %bitcast.5, s32[8,2]{1,0:T(8,128)} %copy.10.shifts, s32[1,8]{1,0:T(1,128)} %valid.1, s32[1]{0:T(128)S(6)} %copy.13.counts, ...), custom_call_target="tpu_custom_call" | custom-call | tf_op jit(solution)/shard_map/difference_coadd/pallas_call | solution.py:336
  56.7 1.3 %copy.14 = f32[1,16,128]{2,1,0:T(8,128)} copy(f32[1,16,128]{2,1,0:T(8,128)} %bitcast.8) | data formatting | bytes 16384
  58.0 1.3 %copy.15 = f32[1,8,45]{2,1,0:T(8,128)} copy(f32[1,8,45]{2,1,0:T(8,128)} %bitcast.9) | data formatting | bytes 2880

commit v3 on v2

--- a/solution.py
+++ b/solution.py
@@ -62,8 +62,6 @@
     for step in (1, tiles - 1):
         near = lax.rem(tile + step, tiles)
         pl.semaphore_signal(barrier, inc=1, device_id=(near, me), device_id_type=MESH)
-    pl.semaphore_wait(barrier, epochs + 1)
-
 
 def dot(a, b):
     return jnp.dot(a, b, preferred_element_type=jnp.float32)
@@ -81,9 +79,9 @@
 def kernel(
     tiles, epochs,
     template, science_hbm, weights_hbm, shifts, valid, counts, col_hbm, row_hbm,
-    coadd_out, coef_out,
+    numer_out, total_out, coef_out,
     science, weights, col_wide, row_wide, ch, cl, rh, rl,
-    own, left, right, fh, fl, basis, lhs, rhs, gram, moved, whole, spill, from_left, from_right, parts,
+    own, left, right, fh, fl, basis, lhs0, rhs0, lhs1, rhs1, gram, moved, whole, spill, from_left, from_right, parts,
     load, send, recv, side_send, side_recv,
 ):
     tile = lax.axis_index("tile")
@@ -103,6 +101,16 @@
     for one in loads:
         one.start()
     greet(tiles, epochs, tile, me)
+    moved[:, 0:SHIFT, :] = jnp.zeros((here, SHIFT, W), jnp.float32)
+    moved[:, SHIFT + H :, :] = jnp.zeros((here, SHIFT, W), jnp.float32)
+    zeros = jnp.zeros((NF, G, W), jnp.bfloat16)
+    for buf in (fh, fl):
+        buf[:, 0:G, :] = zeros
+        buf[:, G + H : G + H + G, :] = zeros
+    gram[...] = jnp.zeros_like(gram)
+    lhs1[...] = jnp.zeros_like(lhs1)
+    rhs1[...] = jnp.zeros_like(rhs1)
+    pl.semaphore_wait(pltpu.get_barrier_semaphore(), epochs + 1)
 
     def to_peers(kind, source, target):
         def copy(step):
@@ -156,14 +164,14 @@
         (valid[0, e] * (me * here + e < counts[0]).astype(jnp.int32)).astype(jnp.float32)
         for e in range(here)
     ]
-    runs = [lax.rem(shifts[e, 1] + W, W) for e in range(here)]
+    runs = [lax.rem(shifts[1, e] + W, W) for e in range(here)]
 
     def gather_sky(field):
         sky = jnp.zeros((H, W), jnp.float32)
         over = jnp.zeros((H, W), jnp.float32)
         for e in range(here):
-            values = moved[e, pl.ds(SHIFT - shifts[e, 0], H), :]
-            origin = lane - shifts[e, 1]
+            values = moved[e, pl.ds(SHIFT - shifts[0, e], H), :]
+            origin = lane - shifts[1, e]
             inside = (origin >= 0) & (origin < W)
             sky += jnp.where(inside, values, 0.0)
             over += jnp.where(inside, 0.0, values)
@@ -187,27 +195,17 @@
 
         return lax.fori_loop(1, epochs, add, whole[field, me])
 
-    moved[:, 0:SHIFT, :] = jnp.zeros((here, SHIFT, W), jnp.float32)
-    moved[:, SHIFT + H :, :] = jnp.zeros((here, SHIFT, W), jnp.float32)
     loads[0].wait()
     for e in range(here):
         moved[e, SHIFT : SHIFT + H, :] = pltpu.roll(lives[e] * weights[e], runs[e], 1)
-    mass_sides = gather_sky(0)
-
-    template_done()
-    tile_sides = to_sides(0, own, left, right)
-    mass_sides()
-    mass_done = merge(0)
-
     loads[1].wait()
     ch[...], cl[...] = halves(col_wide[...])
     loads[2].wait()
     rh[...], rl[...] = halves(row_wide[...])
-    zeros = jnp.zeros((NF, G, W), jnp.bfloat16)
-    for buf in (fh, fl):
-        buf[:, 0:G, :] = zeros
-        buf[:, G + H : G + H + G, :] = zeros
-    gram[...] = jnp.zeros_like(gram)
+
+    template_done()
+    tile_sides = to_sides(0, own, left, right)
+    mass_sides = gather_sky(0)
     tile_sides()
 
     mean = 1.0 / (H * W)
@@ -222,6 +220,8 @@
         fh[f, G : G + H, :] = fhigh
         fl[f, G : G + H, :] = flow
 
+    mass_sides()
+    mass_done = merge(0)
     loads[3].wait()
     turn_to = iota((G * SCI, here * G), 0)
     turn_from = iota((G * SCI, here * G), 1)
@@ -229,7 +229,7 @@
         (turn_to // SCI == turn_from % G) & (turn_to % SCI == turn_from // G)
     ).astype(jnp.float32).astype(jnp.bfloat16)
 
-    def block(i, carry):
+    def make(i, lhs, rhs):
         top = pl.multiple_of(i * G, G)
         pieces = []
         for s in range(NS):
@@ -252,12 +252,21 @@
                 lhs[e * NBP : (e + 1) * NBP, cols] = (
                     wide * weights[e, pl.ds(top + r, 1), :]
                 ).astype(jnp.bfloat16)
+
+    def accumulate(lhs, rhs):
         gram[...] += lax.dot_general(
             lhs[...], rhs[...], (((1,), (1,)), ((), ())), preferred_element_type=jnp.float32
         )
+
+    def blocks(i, carry):
+        accumulate(lhs1, rhs1)
+        make(2 * i, lhs0, rhs0)
+        accumulate(lhs0, rhs0)
+        make(2 * i + 1, lhs1, rhs1)
         return carry
 
-    lax.fori_loop(0, H // G, block, 0)
+    lax.fori_loop(0, H // G // 2, blocks, 0)
+    accumulate(lhs1, rhs1)
 
     eye = (iota((NBP, NBP), 0) == iota((NBP, NBP), 1)).astype(jnp.float32)
     col = iota((NBP, SCI), 1)
@@ -274,22 +283,17 @@
         square = square * (down * across) + RIDGE * eye
         systems.append(jnp.concatenate([square, jnp.where(col == 0, proj, 0.0)], axis=1))
         scales.append(across)
-    a = jnp.stack(systems)
-    row = iota((here, NBP, 1), 1)
-    for k in range(0, NBP, 2):
-        r0, r1 = a[:, k : k + 1, :], a[:, k + 1 : k + 2, :]
-        c0, c1 = a[:, :, k : k + 1], a[:, :, k + 1 : k + 2]
-        p00, p01 = r0[:, :, k : k + 1], r0[:, :, k + 1 : k + 2]
-        p10, p11 = r1[:, :, k : k + 1], r1[:, :, k + 1 : k + 2]
-        inverse = 1.0 / (p00 * p11 - p01 * p10)
-        q0 = (p11 * inverse) * r0 - (p01 * inverse) * r1
-        q1 = (p00 * inverse) * r1 - (p10 * inverse) * r0
-        a = a - (c0 - (row == k).astype(jnp.float32)) * q0 - (c1 - (row == k + 1).astype(jnp.float32)) * q1
-    ys = [jnp.sum(a[e, :, NBP : NBP + 1] * eye, axis=0, keepdims=True) for e in range(here)]
+    rows_of = iota((NBP, 1), 0)
+    for k in [k for k in range(NBP) if k % PER != PER - 1]:
+        unit = (rows_of == k).astype(jnp.float32)
+        for e in range(here):
+            a = systems[e]
+            pivot = a[k : k + 1, :]
+            pivot = pivot * (1.0 / a[k : k + 1, k : k + 1])
+            systems[e] = a - (a[:, k : k + 1] - unit) * pivot
+    ys = [jnp.sum(systems[e][:, NBP : NBP + 1] * eye, axis=0, keepdims=True) for e in range(here)]
     coefs = jnp.concatenate([lives[e] * ys[e] for e in range(here)], axis=0)
-    coef_out[...] = jnp.concatenate(
-        [coefs[:, s * PER : (s + 1) * PER - 1] for s in range(NS)], axis=1
-    )
+    coef_out[...] = coefs
     ks = jnp.concatenate([ys[e] * scales[e] for e in range(here)], axis=0).astype(jnp.bfloat16)
     lanes = iota((NBP, G * NBP), 1)
     spread = (lanes // (G * PER) * PER + lanes % PER == iota((NBP, G * NBP), 0)).astype(jnp.float32).astype(jnp.bfloat16)
@@ -320,9 +324,16 @@
     total = total_of(0)
     prod_sides()
     prod_done = merge(1)
-    root = lax.rsqrt(1.0 + total)
+    total_out[...] = total
     prod_done()
-    coadd_out[...] = total_of(1) * root
+    numer_out[...] = total_of(1)
+
+
+def finish_kernel(numer, total, coefs, coadd_out, coef_out):
+    coadd_out[...] = numer[...] * lax.rsqrt(1.0 + total[...])
+    coef_out[...] = jnp.concatenate(
+        [coefs[:, s * PER : (s + 1) * PER - 1] for s in range(NS)], axis=1
+    )
 
 
 def local(mesh_sizes, template, science, weights, shifts, valid, counts):
@@ -333,14 +344,12 @@
     tile = pltpu.VMEM((H, W), jnp.float32)
     cols = column_taps()
     bands = row_taps()
-    coadd, coefs = pl.pallas_call(
+    coadd_type = jax.ShapeDtypeStruct((rows, W), jnp.float32)
+    sums = pl.pallas_call(
         functools.partial(kernel, tiles, epochs),
-        out_shape=(
-            jax.ShapeDtypeStruct((rows, W), jnp.float32),
-            jax.ShapeDtypeStruct((here, NB), jnp.float32),
-        ),
+        out_shape=(coadd_type, coadd_type, jax.ShapeDtypeStruct((here, NBP), jnp.float32)),
         in_specs=[VMEM, HBM, HBM, SMEM, SMEM, SMEM, HBM, HBM],
-        out_specs=(VMEM, VMEM),
+        out_specs=(VMEM, VMEM, VMEM),
         scratch_shapes=[
             pltpu.VMEM((here, H, W), jnp.bfloat16),
             pltpu.VMEM((here, H, W), jnp.float32),
@@ -356,6 +365,8 @@
             pltpu.VMEM((NF, H + 2 * G, W), jnp.bfloat16),
             pltpu.VMEM((NF, H + 2 * G, W), jnp.bfloat16),
             pltpu.VMEM((H * NBP, W), jnp.bfloat16),
+            pltpu.VMEM((here * NBP, G * W), jnp.bfloat16),
+            pltpu.VMEM((NBP + SCI, G * W), jnp.bfloat16),
             pltpu.VMEM((here * NBP, G * W), jnp.bfloat16),
             pltpu.VMEM((NBP + SCI, G * W), jnp.bfloat16),
             pltpu.VMEM((here * NBP, NBP + SCI), jnp.float32),
@@ -375,7 +386,14 @@
             collective_id=0, has_side_effects=True, vmem_limit_bytes=60 * 1024 * 1024
         ),
         name="difference_coadd",
-    )(template[0], science[0], weights[0], shifts, valid, counts, cols, bands)
+    )(template[0], science[0], weights[0], shifts.T, valid, counts, cols, bands)
+    coadd, coefs = pl.pallas_call(
+        finish_kernel,
+        out_shape=(coadd_type, jax.ShapeDtypeStruct((here, NB), jnp.float32)),
+        in_specs=[VMEM] * 3,
+        out_specs=(VMEM, VMEM),
+        name="finish",
+    )(*sums)
     return (coadd[None], coefs[None])
 
 

time: 59.6 us -> 49.9 us (0.84)
  Pallas kernels: 54.1 us -> 48.4 us
  local copies, waits for them, and re-layouts: 3.91 us -> 0 us
    pallas_call x1 -> x2, Pallas kernels: 54.1 us -> 48.4 us  [the longest x1 47 us: local(): pl.pallas_call(functools.partial(kernel, tiles, epochs), out_shape=(coadd...]
    unnamed x3 -> x0, local copies, waits for them, and re-layouts: 3.91 us -> none
where the time goes in v3:
time: 49.9 us; the launch traced here: 49.7 us
  Pallas kernels  48.4 us (97%)
  between operations  1.29 us (3%)
    pallas_call x1, Pallas kernels, local(): pl.pallas_call(functools.partial(kernel, tiles, epochs), out_shape=(coadd...  47 us
    pallas_call x1, Pallas kernels, local(): pl.pallas_call(finish_kernel, out_shape=(coadd_type, jax.ShapeDtypeStruct...  1.38 us

profile of v3, /device:TPU:0, one launch (start us, length us, event | category | flops | bytes accessed | tf_op | source)
XLA Modules:
  0.0 49.7 jit_solution(16468656571827996123)
XLA Ops:
  1.3 47.0 %difference_coadd.1 = (f32[16,128]{1,0:T(8,128)}, f32[16,128]{1,0:T(8,128)}, f32[8,48]{1,0:T(8,128)}) custom-call(f32[16,128]{1,0:T(8,128)} %bitcast.8, bf16[8,256,128]{2,1,0:T(8,128)(2,1)} %bitcast.7, f32[8,256,128]{2,1,0:T(8,128)} %bitcast.6, s32[2,8]{1,0:T(2,128)} %bitcast.9, s32[1,8]{1,0:T(1,128)} %valid.1, s32[1]{0:T(128)S(6)} %copy.10.counts, ...), custom_call_target="tpu_custom_call" | custom-call | tf_op jit(solution)/shard_map/difference_coadd/pallas_call | solution.py:348
  48.3 1.4 %finish.1 = (f32[16,128]{1,0:T(8,128)}, f32[8,45]{1,0:T(8,128)}) custom-call(f32[16,128]{1,0:T(8,128)} %get-tuple-element.7.numer, f32[16,128]{1,0:T(8,128)} %get-tuple-element.8.total, f32[8,48]{1,0:T(8,128)} %get-tuple-element.9.coefs), custom_call_target="tpu_custom_call" | custom-call | tf_op jit(solution)/shard_map/finish/pallas_call | solution.py:390

commit v4 on v3

--- a/solution.py
+++ b/solution.py
@@ -167,17 +167,20 @@
     runs = [lax.rem(shifts[1, e] + W, W) for e in range(here)]
 
     def gather_sky(field):
-        sky = jnp.zeros((H, W), jnp.float32)
         over = jnp.zeros((H, W), jnp.float32)
         for e in range(here):
-            values = moved[e, pl.ds(SHIFT - shifts[0, e], H), :]
+            origin = lane - shifts[1, e]
+            outside = (origin < 0) | (origin >= W)
+            over += jnp.where(outside, moved[e, pl.ds(SHIFT - shifts[0, e], H), :], 0.0)
+        spill[field] = over.reshape(bands, rows, W)
+        sides = to_sides(1 + field, spill.at[field], from_left.at[field], from_right.at[field])
+        sky = jnp.zeros((H, W), jnp.float32)
+        for e in range(here):
             origin = lane - shifts[1, e]
             inside = (origin >= 0) & (origin < W)
-            sky += jnp.where(inside, values, 0.0)
-            over += jnp.where(inside, 0.0, values)
+            sky += jnp.where(inside, moved[e, pl.ds(SHIFT - shifts[0, e], H), :], 0.0)
         whole[field] = sky.reshape(bands, rows, W)
-        spill[field] = over.reshape(bands, rows, W)
-        return to_sides(1 + field, spill.at[field], from_left.at[field], from_right.at[field])
+        return sides
 
     def merge(field):
         spot = iota((bands, rows, W), 2)
@@ -317,7 +320,7 @@
                 moved[e, spot, :] = pltpu.roll(mass * diff, runs[e], 1)
         return carry
 
-    lax.fori_loop(0, H // G // 2, differ, 0)
+    lax.fori_loop(0, H // G // 2, differ, 0, unroll=4)
 
     prod_sides = gather_sky(1)
     mass_done()

time: 49.9 us -> 48.3 us (0.968)
  Pallas kernels: 48.4 us -> 46.8 us
    pallas_call x1, Pallas kernels: 47 us -> 45.4 us  [local(): pl.pallas_call(functools.partial(kernel, tiles, epochs), out_shape=(coadd...]
where the time goes in v4:
time: 48.3 us; the launch traced here: 48 us
  Pallas kernels  46.8 us (97%)
  between operations  1.29 us (3%)
    pallas_call x1, Pallas kernels, local(): pl.pallas_call(functools.partial(kernel, tiles, epochs), out_shape=(coadd...  45.4 us
    pallas_call x1, Pallas kernels, local(): pl.pallas_call(finish_kernel, out_shape=(coadd_type, jax.ShapeDtypeStruct...  1.38 us

profile of v4, /device:TPU:0, one launch (start us, length us, event | category | flops | bytes accessed | tf_op | source)
XLA Modules:
  0.0 48.0 jit_solution(2000388928151729929)
XLA Ops:
  1.3 45.4 %difference_coadd.1 = (f32[16,128]{1,0:T(8,128)}, f32[16,128]{1,0:T(8,128)}, f32[8,48]{1,0:T(8,128)}) custom-call(f32[16,128]{1,0:T(8,128)} %bitcast.8, bf16[8,256,128]{2,1,0:T(8,128)(2,1)} %bitcast.7, f32[8,256,128]{2,1,0:T(8,128)} %bitcast.6, s32[2,8]{1,0:T(2,128)} %bitcast.9, s32[1,8]{1,0:T(1,128)} %valid.1, s32[1]{0:T(128)S(6)} %copy.10.counts, ...), custom_call_target="tpu_custom_call" | custom-call | tf_op jit(solution)/shard_map/difference_coadd/pallas_call | solution.py:351
  46.7 1.4 %finish.1 = (f32[16,128]{1,0:T(8,128)}, f32[8,45]{1,0:T(8,128)}) custom-call(f32[16,128]{1,0:T(8,128)} %get-tuple-element.7.numer, f32[16,128]{1,0:T(8,128)} %get-tuple-element.8.total, f32[8,48]{1,0:T(8,128)} %get-tuple-element.9.coefs), custom_call_target="tpu_custom_call" | custom-call | tf_op jit(solution)/shard_map/finish/pallas_call | solution.py:393
